TPU v7x, 768 devices: a whole 4x8x12 slice. The times are simulated.
768 devices in a mesh: node: 96 (over x, z, core), local: 8 (over y).
Axes of the slice: x: 4, y: 8, z: 12, core: 2. Of those that a mesh axis runs over, the one named last changes fastest.
Arguments:
- image: float32 [12288, 128], P(('node', 'local')), may hold values from -6 to 6
- direction: float32 [12288, 128], P(('node', 'local')), may hold values from -60 to 60
- gradient: float32 [12288, 128], P(('node', 'local')), may hold values from -60 to 60
- residual: float32 [6144, 128], P(('node', 'local')), may hold values from -6 to 6
- blocks: bfloat16 [24576, 128, 128], P(('node', 'local')), may hold values from -0.25 to 0.25
- block_slot: int32 [24576], P(('node', 'local')), may hold values from 0 to 767
- block_pixel: int32 [24576], P(('node', 'local')), may hold values from 0 to 15
- slot_ray: int32 [73728], P(('node', 'local')), may hold values from 0 to 6143, as said below
Outputs:
- new_image: float32 [12288, 128], P(('node', 'local'))
- new_residual: float32 [6144, 128], P(('node', 'local'))
- new_direction: float32 [12288, 128], P(('node', 'local'))
Inputs may be any that keep to these rules, and one draw needn't show every extreme that they name: `slot_ray`: slot j of device d (entry d * 96 + j) names a ray tile owned by a device with the same index along local as d (ray tile t is owned by device t // 8). From one device at most 2 slots name ray tiles owned by the devices of one index along node, exactly 2 for some index, and for every index along local some owner receives exactly 2 slots from every device of that local index.
All inputs are finite; a program needn't handle non-finite values.
Results may differ from a plain program's by a relative error of at most 0.0028.
Values may be sent and summed in bfloat16 or wider, within the bound.
A program may use at most 32 MiB of HBM per device.

v0:
```python
import jax
import jax.numpy as jnp
from jax import lax
from jax.sharding import PartitionSpec as P

SEND_CAPACITY = 2


def slot_positions(targets, stride):
    length_rows = targets.shape[0]
    matching = targets[:, None] == targets[None, :]
    earlier = jnp.arange(length_rows)[None, :] < jnp.arange(length_rows)[:, None]
    standing = jnp.sum((matching & earlier).astype(jnp.int32), axis=1)
    return targets * stride + standing


def spread_matrix(position, slots_total):
    return (jnp.arange(slots_total, dtype=jnp.int32)[:, None] == position[None, :]).astype(
        jnp.float32
    )


def on_device(image, direction, gradient, residual, blocks, block_slot, block_pixel, slot_ray):
    node_count = lax.axis_size("node")
    local_count = lax.axis_size("local")
    held_slots = slot_ray.shape[0]
    owned_rays = residual.shape[0]
    pixel_tiles = image.shape[0]
    norm_part = jnp.sum(gradient * gradient)
    norm_old = lax.psum(norm_part, ("node", "local"))
    low_dir = direction.astype(jnp.bfloat16)
    contrib = jnp.einsum(
        "brp,bp->br", blocks, low_dir[block_pixel], preferred_element_type=jnp.float32
    )
    partial_value = jax.ops.segment_sum(contrib, block_slot, num_segments=held_slots * local_count)
    held_sums = lax.psum_scatter(partial_value, "local", scatter_dimension=0, tiled=True)
    owner_device = slot_ray // owned_rays
    target_node = owner_device // local_count
    tile_position = slot_ray % owned_rays
    spread = spread_matrix(slot_positions(target_node, SEND_CAPACITY), node_count * SEND_CAPACITY)
    send_rows = jnp.dot(spread, held_sums, precision=lax.Precision.HIGHEST)
    send_labels = jnp.dot(
        spread, (tile_position + 1).astype(jnp.float32), precision=lax.Precision.HIGHEST
    )
    received, received_labels = (
        lax.all_to_all(send_rows, "node", split_axis=0, concat_axis=0, tiled=True),
        lax.all_to_all(send_labels, "node", split_axis=0, concat_axis=0, tiled=True),
    )
    select = (
        received_labels[:, None] == (jnp.arange(owned_rays) + 1).astype(jnp.float32)[None, :]
    ).astype(jnp.float32)
    projected = jnp.dot(select.T, received, precision=lax.Precision.HIGHEST)
    curve_part = jnp.sum(projected * projected)
    curvature = lax.psum(curve_part, ("node", "local"))
    step_size = norm_old / curvature
    new_image = image + step_size * direction
    new_residual = residual - step_size * projected
    reply_rows = jnp.dot(select, new_residual, precision=lax.Precision.HIGHEST).astype(jnp.bfloat16)
    returned = lax.all_to_all(reply_rows, "node", split_axis=0, concat_axis=0, tiled=True)
    held_residual = jnp.dot(
        spread.T.astype(jnp.bfloat16), returned, preferred_element_type=jnp.float32
    ).astype(jnp.bfloat16)
    group_res = lax.all_gather(held_residual, "local", axis=0, tiled=True)
    chosen = group_res[block_slot]
    backward = jnp.einsum("brp,br->bp", blocks, chosen, preferred_element_type=jnp.float32)
    gradient_new = jax.ops.segment_sum(backward, block_pixel, num_segments=pixel_tiles)
    norm_new = lax.psum(jnp.sum(gradient_new * gradient_new), ("node", "local"))
    new_direction = gradient_new + norm_new / norm_old * direction
    return (new_image, new_residual, new_direction)


def solution(mesh):
    return jax.shard_map(
        on_device,
        mesh=mesh,
        in_specs=(
            P(("node", "local"), None),
            P(("node", "local"), None),
            P(("node", "local"), None),
            P(("node", "local"), None),
            P(("node", "local"), None, None),
            P(("node", "local")),
            P(("node", "local")),
            P(("node", "local")),
        ),
        out_specs=(
            P(("node", "local"), None),
            P(("node", "local"), None),
            P(("node", "local"), None),
        ),
        check_vma=False,
    )
```

profile of v0, /device:TPU:1, one launch (start us, length us, event | category | flops | bytes accessed | tf_op | source)
XLA Modules:
  0.0 358.3 jit_solution(15661764716402258816)
XLA Ops:
  7.2 0.0 copy-start
  7.2 0.0 copy-start.8
  7.2 0.0 reduce-scatter.2.cloned.1.call-start
  7.2 0.8 convert_element_type.33
  8.0 0.0 copy-done.8
  8.0 0.6 gather_fusion
  8.6 0.0 copy-done
  8.6 0.6 fusion.17
  9.3 0.0 copy-start.7
  9.3 0.7 copy-done.7
  9.9 1.4 scatter_custom_fusion
  11.4 0.0 copy-start.6
  11.4 0.0 reduce-scatter.2.cloned.1.call-update
  11.4 0.6 copy-done.6
  12.0 0.2 convert_reduce_fusion
  12.2 0.1 fusion.6
  12.4 0.8 all_to_all.22
  13.2 20.0 %all-to-all-start = ((f32[96,2,1]{1,2,0:T(1,128)}), f32[96,2,1]{1,2,0:T(1,128)S(1)}, u32[]{:S(2)}, u32[]{:S(2)}) async-start(f32[96,2,1]{1,2,0:T(1,128)} %bitcast.2), calls=%async_computation | async-start | bytes 98304 | tf_op jit(solution)/shard_map/all_to_all | solution.py:47
  33.3 23.7 %reduce-scatter.2.cloned.1.call-done = f32[96,128]{1,0:T(8,128)} async-done(((f32[768,128]{1,0:T(8,128)}), f32[96,128]{1,0:T(8,128)}) %reduce-scatter.2.cloned.1.call-update) | async-done | bytes 49168 | tf_op jit(solution)/shard_map/reduce_scatter | solution.py:36
  56.9 1.6 fusion.5
  58.6 0.0 all-to-all-done
  58.6 0.0 copy-start.2
  58.6 18.5 %all-to-all-start.1 = ((f32[96,2,128]{2,1,0:T(2,128)}), f32[96,2,128]{2,1,0:T(2,128)S(1)}, u32[]{:S(2)}, u32[]{:S(2)}) async-start(f32[96,2,128]{2,1,0:T(2,128)} %bitcast.6), calls=%async_computation.2 | async-start | bytes 196608 | tf_op jit(solution)/shard_map/all_to_all | solution.py:46
  77.1 0.0 copy-done.2
  77.1 0.6 multiply_reduce_fusion.1
  77.7 0.5 broadcast.68
  78.2 0.8 reduce.3
  79.0 0.1 eq.56
  79.1 11.4 %all-to-all-done.1 = f32[96,2,128]{2,1,0:T(2,128)S(1)} async-done(((f32[96,2,128]{2,1,0:T(2,128)}), f32[96,2,128]{2,1,0:T(2,128)S(1)}, u32[]{:S(2)}, u32[]{:S(2)}) %all-to-all-start.1) | async-done | bytes 98336 | tf_op jit(solution)/shard_map/all_to_all | solution.py:46
  90.5 0.9 multiply_reduce_fusion.2
  91.4 104.5 %all-reduce = (f32[]{:T(128)}, f32[]{:T(128)}) all-reduce(f32[]{:T(128)} %multiply_reduce_fusion.1, f32[]{:T(128)} %get-tuple-element.7), channel_id=1, replica_groups=mesh['node'=96,'local'=8] {'node','local'}, use_global_device_ids=true, to_apply=%region_1.0 | all-reduce | flops 2 | bytes 16 | tf_op jit(solution)/shard_map/psum | solution.py:30
  196.0 0.0 copy-start.4
  197.3 0.0 copy-done.4
  197.4 0.0 copy-start.5
  197.4 0.9 convolution_convert_fusion
  198.2 0.0 copy-done.5
  198.2 7.3 %all-to-all-start.2 = ((bf16[96,2,128]{2,1,0:T(2,128)(2,1)}), bf16[96,2,128]{2,1,0:T(2,128)(2,1)S(1)}, u32[]{:S(2)}, u32[]{:S(2)}) async-start(bf16[96,2,128]{2,1,0:T(2,128)(2,1)} %bitcast.8), calls=%async_computation.3 | async-start | bytes 98304 | tf_op jit(solution)/shard_map/all_to_all | solution.py:59
  205.6 12.2 %all-to-all-done.2 = bf16[96,2,128]{2,1,0:T(2,128)(2,1)S(1)} async-done(((bf16[96,2,128]{2,1,0:T(2,128)(2,1)}), bf16[96,2,128]{2,1,0:T(2,128)(2,1)S(1)}, u32[]{:S(2)}, u32[]{:S(2)}) %all-to-all-start.2) | async-done | bytes 49184 | tf_op jit(solution)/shard_map/all_to_all | solution.py:59
  217.8 0.2 convolution_convert_fusion.1
  217.9 19.5 %all_gather.3 = bf16[768,128]{1,0:T(8,128)(2,1)S(1)} all-gather(bf16[96,128]{1,0:T(8,128)(2,1)S(1)} %convolution_convert_fusion.1), channel_id=1, replica_groups=mesh['node'=96,'local'=8] {'local'}, dimensions={0}, use_global_device_ids=true | all-gather | bytes 221184 | tf_op jit(solution)/shard_map/all_gather | solution.py:63
  237.5 0.6 gather_fusion.1
  238.1 0.4 fusion.15
  238.5 0.0 copy-start.3
  238.5 0.7 scatter_custom_fusion.1
  239.2 0.0 copy-start.1
  239.2 0.6 multiply_reduce_fusion
  239.8 109.7 %psum.23 = f32[]{:T(128)} all-reduce(f32[]{:T(128)} %multiply_reduce_fusion), channel_id=1, replica_groups=mesh['node'=96,'local'=8] {'node','local'}, use_global_device_ids=true, to_apply=%region_9.10 | all-reduce | flops 1 | bytes 8 | tf_op jit(solution)/shard_map/psum | solution.py:67
  350.8 0.0 copy-done.3
  350.9 0.0 copy-done.1
  350.9 0.6 multiply_add_fusion
  (8 shorter events, 0.1 us)
Async XLA Ops:
  7.2 1.5 copy-start
  7.2 0.8 copy-start.8
  7.2 49.8 %reduce-scatter.2.cloned.1.call-start = ((), (), s32[]{:S(2)}) async-start(), calls=%async_computation.4 | async-start | bytes 442368 | tf_op jit(solution)/shard_map/reduce_scatter | solution.py:36
  9.3 0.7 copy-start.7
  11.4 0.7 copy-start.6
  13.2 45.3 %all-to-all-start = ((f32[96,2,1]{1,2,0:T(1,128)}), f32[96,2,1]{1,2,0:T(1,128)S(1)}, u32[]{:S(2)}, u32[]{:S(2)}) async-start(f32[96,2,1]{1,2,0:T(1,128)} %bitcast.2), calls=%async_computation | async-start | bytes 98304 | tf_op jit(solution)/shard_map/all_to_all | solution.py:47
  58.6 18.5 %copy-start.2 = (f32[16,128]{1,0:T(8,128)S(1)}, f32[16,128]{1,0:T(8,128)}, u32[]{:S(2)}) copy-start(f32[16,128]{1,0:T(8,128)} %param.10) | copy-start | bytes 24580
  58.6 32.0 %all-to-all-start.1 = ((f32[96,2,128]{2,1,0:T(2,128)}), f32[96,2,128]{2,1,0:T(2,128)S(1)}, u32[]{:S(2)}, u32[]{:S(2)}) async-start(f32[96,2,128]{2,1,0:T(2,128)} %bitcast.6), calls=%async_computation.2 | async-start | bytes 196608 | tf_op jit(solution)/shard_map/all_to_all | solution.py:46
  196.0 1.4 copy-start.4
  197.4 0.9 copy-start.5
  198.2 19.5 %all-to-all-start.2 = ((bf16[96,2,128]{2,1,0:T(2,128)(2,1)}), bf16[96,2,128]{2,1,0:T(2,128)(2,1)S(1)}, u32[]{:S(2)}, u32[]{:S(2)}) async-start(bf16[96,2,128]{2,1,0:T(2,128)(2,1)} %bitcast.8), calls=%async_computation.3 | async-start | bytes 98304 | tf_op jit(solution)/shard_map/all_to_all | solution.py:59
  238.5 112.4 %copy-start.3 = (f32[16,128]{1,0:T(8,128)S(1)}, f32[16,128]{1,0:T(8,128)}, u32[]{:S(2)}) copy-start(f32[16,128]{1,0:T(8,128)} %param.8) | copy-start | bytes 24580
  239.2 111.7 %copy-start.1 = (f32[16,128]{1,0:T(8,128)S(1)}, f32[16,128]{1,0:T(8,128)}, u32[]{:S(2)}) copy-start(f32[16,128]{1,0:T(8,128)} %param.9) | copy-start | bytes 24580
Sparse Core Ops, SparseCore 0:
  11.5 45.4 reduce-scatter.1
where the time goes:
time: 359 us; the launch traced here: 358 us
  blocking collectives  234 us (65%)
  waiting for transfers between devices  47.3 us (13%)
  starting transfers between devices  45.9 us (13%)
  between operations  16.9 us (5%)
  other arithmetic  5.7 us (2%)
  matrix products  4.71 us (1%)
  local copies, waits for them, and re-layouts  4.02 us (1%)
    psum x1, blocking collectives, on_device(): norm_new = lax.psum(jnp.sum(gradient_new * gradient_new), ('node', 'local'))  110 us
    psum x1, blocking collectives, on_device(): norm_old = lax.psum(norm_part, ('node', 'local'))  105 us
    reduce_scatter x1, waiting for transfers between devices, on_device(): lax.psum_scatter(partial_value, 'local', scatter_dimension=0, tiled=True)  23.7 us
    all_to_all x1, starting transfers between devices, on_device(): lax.all_to_all(send_labels, 'node', split_axis=0, concat_axis=0, tiled=True)  20 us
    all_gather x1, blocking collectives, on_device(): group_res = lax.all_gather(held_residual, 'local', axis=0, tiled=True)  19.5 us
    all_to_all x1, starting transfers between devices, on_device(): lax.all_to_all(send_rows, 'node', split_axis=0, concat_axis=0, tiled=True)  18.5 us
    all_to_all x1, waiting for transfers between devices, on_device(): lax.all_to_all(reply_rows, 'node', split_axis=0, concat_axis=0, tiled=True)  12.2 us
    all_to_all x1, waiting for transfers between devices, on_device(): lax.all_to_all(send_rows, 'node', split_axis=0, concat_axis=0, tiled=True)  11.4 us
  transfers between devices with their start and end apart: 4, of which 3 were waited for; matrix products, arithmetic and copies ran while one was open for 1% of the time, Pallas kernels for 0%

commit v1 on v0

v1 whole, which is shorter than its diff:
```python
import functools

import jax
import jax.numpy as jnp
from jax import lax
from jax.experimental import pallas as pl
from jax.experimental.pallas import tpu as pltpu
from jax.sharding import PartitionSpec as P

SEND_CAPACITY = 2
LANES = 128
MESH = pl.DeviceIdType.MESH
NT = (((1,), (1,)), ((), ()))


def iota(shape, axis):
    return lax.broadcasted_iota(jnp.int32, shape, axis)


def dot(a, b, dims=(((1,), (0,)), ((), ()))):
    return lax.dot_general(a, b, dims, preferred_element_type=jnp.float32)


def one_hot_dot(one_hot, value):
    high = value.astype(jnp.bfloat16)
    rest = value - high.astype(jnp.float32)
    middle = rest.astype(jnp.bfloat16)
    low = (rest - middle.astype(jnp.float32)).astype(jnp.bfloat16)
    width = value.shape[1]
    out = dot(one_hot, jnp.concatenate([high, middle, low], axis=1))
    return out[:, :width] + (out[:, width : 2 * width] + out[:, 2 * width :])


def to_column(row):
    length = row.shape[1]
    square = (length, length)
    return jnp.sum(jnp.where(iota(square, 0) == iota(square, 1), row, 0.0), axis=1, keepdims=True)


def kernel(
    sizes,
    image_hbm, direction_hbm, gradient_hbm, residual_hbm, blocks_hbm, slot_hbm, pixel_hbm, ray_hbm,
    image_out, residual_out, direction_out,
    image, direction, gradient, residual, blocks, slot, pixel, ray, load_sem,
    slot_send, slot_recv, label_send, label_recv,
    contrib_send, contrib_recv, held_send, held_recv,
    reply_send, reply_recv, chosen_send, chosen_recv,
    early_send, early_recv, early_chosen_send, early_chosen_recv,
    norm_a_send, norm_a_recv, norm_b_send, norm_b_recv,
    last_a_send, last_a_recv, last_b_send, last_b_recv,
    y_send_sem, y_recv_sem, n_send_sem, n_recv_sem, s_send_sem, s_recv_sem,
):
    node_count, local_count, row_count = sizes
    column_count = node_count // row_count
    node = lax.axis_index("node")
    local = lax.axis_index("local")
    row = node // column_count
    column = lax.rem(node, column_count)
    tiles, block_count = image.shape[0], blocks.shape[0]
    held, owned = ray.shape[1], residual.shape[0]
    rows_sent = node_count * SEND_CAPACITY
    group_blocks = block_count * local_count

    chunks = 4
    chunk = block_count // chunks
    loads = {}
    for index, (name, source, target) in enumerate(
        (
            ("ray", ray_hbm, ray),
            ("direction", direction_hbm, direction),
            ("pixel", pixel_hbm, pixel),
            ("slot", slot_hbm, slot),
            *(
                (("blocks", c), blocks_hbm.at[pl.ds(c * chunk, chunk)], blocks.at[pl.ds(c * chunk, chunk)])
                for c in range(chunks)
            ),
            ("gradient", gradient_hbm, gradient),
            ("residual", residual_hbm, residual),
            ("image", image_hbm, image),
        )
    ):
        loads[name] = pltpu.make_async_copy(source, target, load_sem.at[index])
        loads[name].start()

    def of_local(k):
        other = lax.rem(local + k, local_count)
        return other, (node, other)

    def of_node(k):
        other = lax.rem(node + k, node_count)
        return other, (other, local)

    def of_column(k):
        other = lax.rem(column + k, column_count)
        return other, (row * column_count + other, local)

    def of_plane(k):
        me = row * local_count + local
        other = lax.rem(me + k, row_count * local_count)
        return other, (other // local_count * column_count + column, lax.rem(other, local_count))

    local_group = (local_count, local, of_local)
    node_group = (node_count, node, of_node)
    column_group = (column_count, column, of_column)
    plane_group = (row_count * local_count, row * local_count + local, of_plane)

    def each(group, body):
        def step(k, carry):
            body(*group[2](k))
            return carry

        lax.fori_loop(1, group[0], step, 0)

    barrier = pltpu.get_barrier_semaphore()
    for group in (local_group, node_group, plane_group):
        each(group, lambda other, device: pl.semaphore_signal(barrier, inc=1, device_id=device, device_id_type=MESH))

    def exchange(group, source, target, send_sem, recv_sem):
        def send(other, device):
            pltpu.make_async_remote_copy(
                src_ref=source(other), dst_ref=target, send_sem=send_sem, recv_sem=recv_sem,
                device_id=device, device_id_type=MESH,
            ).start()

        each(group, send)
        pltpu.make_async_copy(source(group[1]), target, recv_sem).start()

    def arrived(buffer, recv_sem):
        pltpu.make_async_copy(buffer, buffer, recv_sem).wait()

    loads["ray"].wait()
    rays = ray[...]
    target_node = lax.div(rays, owned * local_count).astype(jnp.float32)
    tile = lax.rem(rays, owned).astype(jnp.float32)
    square = (held, held)
    standing = jnp.sum(
        jnp.where((to_column(target_node) == target_node) & (iota(square, 0) < iota(square, 1)), 1.0, 0.0),
        axis=0,
        keepdims=True,
    )
    position = target_node * SEND_CAPACITY + standing
    spread = (iota((rows_sent, held), 0).astype(jnp.float32) == position).astype(jnp.bfloat16)
    tile_one_hot = (iota((held, LANES), 1).astype(jnp.float32) == to_column(tile)).astype(jnp.bfloat16)
    label_send[...] = dot(spread, tile_one_hot)

    loads["slot"].wait()
    slot_row = jnp.concatenate([slot[...].astype(jnp.float32)] * local_count, axis=1)
    slot_send[...] = jnp.where(iota(slot_row.shape, 1) // block_count == local, slot_row, 0.0)

    loads["direction"].wait()
    loads["pixel"].wait()
    low_direction = direction[...].astype(jnp.bfloat16)
    tile_index = iota((tiles, LANES), 0)
    for c in range(chunks):
        loads["blocks", c].wait()
        chunk_blocks = blocks[pl.ds(c * chunk, chunk)].reshape(chunk * LANES, LANES)
        products = dot(low_direction, chunk_blocks, NT)
        for i in range(chunk):
            b = c * chunk + i
            mine = jnp.where(tile_index == pixel[0, b], products[:, i * LANES : (i + 1) * LANES], 0.0)
            contrib_send[pl.ds(b, 1), :] = jnp.sum(mine, axis=0, keepdims=True)

    pl.semaphore_wait(barrier, local_count + node_count + row_count * local_count - 3)

    my_blocks = pl.ds(pl.multiple_of(local * block_count, block_count), block_count)
    my_rows = pl.ds(node * SEND_CAPACITY, SEND_CAPACITY)

    def rows_of(buffer):
        return lambda other: buffer.at[pl.ds(other * SEND_CAPACITY, SEND_CAPACITY)]

    def blocks_of(buffer):
        return lambda other: buffer.at[pl.ds(pl.multiple_of(other * block_count, block_count), block_count)]

    exchange(local_group, lambda other: contrib_send, contrib_recv.at[my_blocks], y_send_sem.at[1], y_recv_sem.at[1])
    exchange(local_group, lambda other: slot_send, slot_recv.at[local], y_send_sem.at[0], y_recv_sem.at[0])
    exchange(node_group, rows_of(label_send), label_recv.at[my_rows], n_send_sem.at[0], n_recv_sem.at[0])

    arrived(slot_recv, y_recv_sem.at[0])
    group_slot = jnp.sum(slot_recv[...], axis=0) - (local * held).astype(jnp.float32)
    in_slot = (iota((held, group_blocks), 0).astype(jnp.float32) == group_slot).astype(jnp.bfloat16)
    of_slot = (iota((group_blocks, held), 1).astype(jnp.float32) == to_column(group_slot)).astype(jnp.bfloat16)
    gather_rows = dot(spread, in_slot).astype(jnp.bfloat16)
    scatter_rows = dot(of_slot, spread, NT).astype(jnp.bfloat16)

    arrived(contrib_recv, y_recv_sem.at[1])
    held_send[...] = one_hot_dot(gather_rows, contrib_recv[...])
    exchange(node_group, rows_of(held_send), held_recv.at[my_rows], n_send_sem.at[1], n_recv_sem.at[1])

    arrived(label_recv, n_recv_sem.at[0])
    labels = label_recv[...].astype(jnp.bfloat16)
    tile_square = (iota((owned, LANES), 0) == iota((owned, LANES), 1)).astype(jnp.bfloat16)
    collect = dot(tile_square, labels, NT).astype(jnp.bfloat16)
    labels_owned = labels[:, :owned]
    loads["residual"].wait()
    early_send[...] = one_hot_dot(labels_owned, residual[...])
    exchange(node_group, rows_of(early_send), early_recv.at[my_rows], n_send_sem.at[2], n_recv_sem.at[2])

    loads["gradient"].wait()
    loads["image"].wait()
    old_norm_row = jnp.sum(gradient[...] * gradient[...], axis=0, keepdims=True)

    arrived(held_recv, n_recv_sem.at[1])
    projected = one_hot_dot(collect, held_recv[...])
    reply_send[...] = one_hot_dot(labels_owned, projected)
    exchange(node_group, rows_of(reply_send), reply_recv.at[my_rows], n_send_sem.at[3], n_recv_sem.at[3])
    norm_a_send[0:1, :] = jnp.sum(projected * projected, axis=0, keepdims=True)
    norm_a_send[1:2, :] = old_norm_row
    exchange(column_group, lambda other: norm_a_send, norm_a_recv.at[column], s_send_sem.at[0], s_recv_sem.at[0])

    arrived(early_recv, n_recv_sem.at[2])
    early_chosen_send[...] = one_hot_dot(scatter_rows, early_recv[...])
    exchange(
        local_group, blocks_of(early_chosen_send), early_chosen_recv.at[local], y_send_sem.at[2], y_recv_sem.at[2]
    )

    arrived(norm_a_recv, s_recv_sem.at[0])
    norm_b_send[...] = jnp.sum(norm_a_recv[...], axis=0)
    me_in_plane = plane_group[1]
    exchange(plane_group, lambda other: norm_b_send, norm_b_recv.at[me_in_plane], s_send_sem.at[1], s_recv_sem.at[1])

    arrived(reply_recv, n_recv_sem.at[3])
    chosen_send[...] = one_hot_dot(scatter_rows, reply_recv[...])
    exchange(local_group, blocks_of(chosen_send), chosen_recv.at[local], y_send_sem.at[3], y_recv_sem.at[3])

    arrived(norm_b_recv, s_recv_sem.at[1])
    norms = jnp.sum(norm_b_recv[...], axis=0)
    curvature = jnp.sum(norms[0:1, :], axis=1, keepdims=True)
    old_norm = jnp.sum(norms[1:2, :], axis=1, keepdims=True)
    step_size = old_norm / curvature
    image_out[...] = image[...] + step_size * direction[...]
    residual_out[...] = residual[...] - step_size * projected

    arrived(early_chosen_recv, y_recv_sem.at[2])
    old_chosen = jnp.sum(early_chosen_recv[...], axis=0)
    arrived(chosen_recv, y_recv_sem.at[3])
    chosen = old_chosen - step_size * jnp.sum(chosen_recv[...], axis=0)

    gradient_new = jnp.zeros((tiles, LANES), jnp.float32)
    for c in range(chunks):
        spread_residual = jnp.concatenate(
            [
                jnp.where(tile_index == pixel[0, b], chosen[b : b + 1, :], 0.0)
                for b in range(c * chunk, (c + 1) * chunk)
            ],
            axis=1,
        ).astype(jnp.bfloat16)
        chunk_blocks = blocks[pl.ds(c * chunk, chunk)].reshape(chunk * LANES, LANES)
        gradient_new += dot(spread_residual, chunk_blocks)

    last_a_send[...] = jnp.sum(gradient_new * gradient_new, axis=0, keepdims=True)
    exchange(column_group, lambda other: last_a_send, last_a_recv.at[column], s_send_sem.at[2], s_recv_sem.at[2])
    arrived(last_a_recv, s_recv_sem.at[2])
    last_b_send[...] = jnp.sum(last_a_recv[...], axis=0)
    exchange(plane_group, lambda other: last_b_send, last_b_recv.at[me_in_plane], s_send_sem.at[3], s_recv_sem.at[3])
    arrived(last_b_recv, s_recv_sem.at[3])
    new_norm = jnp.sum(jnp.sum(last_b_recv[...], axis=0), axis=1, keepdims=True)
    direction_out[...] = gradient_new + (new_norm / old_norm) * direction[...]

    def sent(group, buffer, each_rows, send_sem):
        sample = buffer.at[pl.ds(0, (group[0] - 1) * each_rows)]
        pltpu.make_async_copy(sample, sample, send_sem).wait()

    sent(local_group, slot_recv, 1, y_send_sem.at[0])
    sent(local_group, contrib_recv, block_count, y_send_sem.at[1])
    sent(local_group, early_chosen_recv, 1, y_send_sem.at[2])
    sent(local_group, chosen_recv, 1, y_send_sem.at[3])
    for index, buffer in enumerate((label_recv, held_recv, early_recv, reply_recv)):
        sent(node_group, buffer, SEND_CAPACITY, n_send_sem.at[index])
    sent(column_group, norm_a_recv, 1, s_send_sem.at[0])
    sent(plane_group, norm_b_recv, 1, s_send_sem.at[1])
    sent(column_group, last_a_recv, 1, s_send_sem.at[2])
    sent(plane_group, last_b_recv, 1, s_send_sem.at[3])


def solution(mesh):
    node_count, local_count = mesh.shape["node"], mesh.shape["local"]
    row_count = 4 if node_count % 4 == 0 and node_count > 4 else 2
    column_count = node_count // row_count
    plane_count = row_count * local_count

    def on_device(image, direction, gradient, residual, blocks, block_slot, block_pixel, slot_ray):
        rows_sent = node_count * SEND_CAPACITY
        block_count, held = block_slot.shape[0], slot_ray.shape[0]
        group_blocks = block_count * local_count
        chosen_shape = (local_count, block_count, LANES)

        def f32(*shape):
            return pltpu.VMEM(shape, jnp.float32)

        def pair(send, recv):
            return [f32(*send), f32(*recv)]

        rows, group = (rows_sent, LANES), (group_blocks, LANES)
        scratch = [
            f32(*image.shape), f32(*image.shape), f32(*image.shape), f32(*residual.shape),
            pltpu.VMEM(blocks.shape, jnp.bfloat16), pltpu.VMEM((1, block_count), jnp.int32),
            pltpu.SMEM((1, block_count), jnp.int32), pltpu.VMEM((1, held), jnp.int32),
            pltpu.SemaphoreType.DMA((11,)),
            *pair((1, group_blocks), (local_count, 1, group_blocks)),
            *pair(rows, rows),
            *pair((block_count, LANES), group),
            *pair(rows, rows),
            *pair(rows, rows),
            *pair(group, chosen_shape),
            *pair(rows, rows),
            *pair(group, chosen_shape),
            *pair((2, LANES), (column_count, 2, LANES)),
            *pair((2, LANES), (plane_count, 2, LANES)),
            *pair((1, LANES), (column_count, 1, LANES)),
            *pair((1, LANES), (plane_count, 1, LANES)),
            *[pltpu.SemaphoreType.DMA((4,))] * 6,
        ]
        return pl.pallas_call(
            functools.partial(kernel, (node_count, local_count, row_count)),
            out_shape=tuple(jax.ShapeDtypeStruct(a.shape, jnp.float32) for a in (image, residual, direction)),
            in_specs=[pl.BlockSpec(memory_space=pl.ANY)] * 8,
            out_specs=[pl.BlockSpec(memory_space=pltpu.VMEM)] * 3,
            scratch_shapes=scratch,
            compiler_params=pltpu.CompilerParams(
                collective_id=0, has_side_effects=True, vmem_limit_bytes=32 * 1024 * 1024
            ),
        )(
            image, direction, gradient, residual, blocks,
            block_slot.reshape(1, block_count), block_pixel.reshape(1, block_count), slot_ray.reshape(1, held),
        )

    split = P(("node", "local"))
    return jax.shard_map(
        on_device,
        mesh=mesh,
        in_specs=(split,) * 8,
        out_specs=(split,) * 3,
        check_vma=False,
    )
```

time: 359 us -> 74 us (0.21)
  blocking collectives: 234 us -> 0 us
  Pallas kernels: 0 us -> 67.2 us
  waiting for transfers between devices: 47.3 us -> 0 us
  starting transfers between devices: 45.9 us -> 0 us
  between operations: 16.9 us -> 0.68 us
  other arithmetic: 5.7 us -> 0 us
  matrix products: 4.71 us -> 0 us
    psum x2 -> x0, blocking collectives: 214 us -> none  [the longest x1 110 us: on_device(): norm_new = lax.psum(jnp.sum(gradient_new * gradient_new), ('node', 'local'))]
    pallas_call x0 -> x1, Pallas kernels: none -> 67.2 us  [on_device(): pl.pallas_call(functools.partial(kernel, (node_count, local_count, row_co...]
    all_to_all x3 -> x0, starting transfers between devices: 45.9 us -> none  [the longest x1 20 us: on_device(): lax.all_to_all(send_labels, 'node', split_axis=0, concat_axis=0, tiled=True)]
    reduce_scatter x1 -> x0, waiting for transfers between devices: 23.7 us -> none  [on_device(): lax.psum_scatter(partial_value, 'local', scatter_dimension=0, tiled=True)]
    all_to_all x3 -> x0, waiting for transfers between devices: 23.6 us -> none  [the longest x1 12.2 us: on_device(): lax.all_to_all(reply_rows, 'node', split_axis=0, concat_axis=0, tiled=True)]
    all_gather x1 -> x0, blocking collectives: 19.5 us -> none  [on_device(): group_res = lax.all_gather(held_residual, 'local', axis=0, tiled=True)]
    dot_general x7 -> x0, matrix products: 4.71 us -> none  [the longest x1 1.61 us: on_device(): send_rows = jnp.dot(spread, held_sums, precision=lax.Precision.HIGHEST)]
    unnamed x18 -> x19, local copies, waits for them, and re-layouts: 1.34 us -> 5.77 us
  transfers between devices with their start and end apart: 4 -> 0, of which waited for: 3 -> 0; matrix products, arithmetic and copies ran while one was open for 1% -> 0% of each run, Pallas kernels for 0% -> 0%
where the time goes in v1:
time: 74 us; the launch traced here: 73.7 us
  Pallas kernels  67.2 us (91%)
  local copies, waits for them, and re-layouts  5.77 us (8%)
    pallas_call x1, Pallas kernels, on_device(): pl.pallas_call(functools.partial(kernel, (node_count, local_count, row_co...  67.2 us
    unnamed x19, local copies, waits for them, and re-layouts  5.77 us

profile of v1, /device:TPU:1, one launch (start us, length us, event | category | flops | bytes accessed | tf_op | source)
XLA Modules:
  0.0 73.7 jit_solution(15858992351664578782)
XLA Ops:
  0.6 0.0 copy-start.4
  0.6 0.0 copy-start.5
  0.7 0.0 copy-start.6
  0.7 0.0 copy-start.7
  0.7 0.6 copy-done.4
  1.3 0.0 copy-done.5
  1.3 0.0 copy-done.6
  1.3 0.0 copy-done.7
  1.3 0.0 copy-start
  1.3 1.2 %copy-done = bf16[32,128,128]{2,1,0:T(8,128)(2,1)S(1)} copy-done((bf16[32,128,128]{2,1,0:T(8,128)(2,1)S(1)}, bf16[32,128,128]{2,1,0:T(8,128)(2,1)}, u32[]{:S(2)}) %copy-start) | copy-done | bytes 1048600
  2.6 0.0 copy-start.1
  2.6 0.7 copy-done.1
  3.3 0.0 copy-start.2
  3.3 0.7 copy-done.2
  4.0 0.0 copy-start.3
  4.0 0.7 copy-done.3
  4.7 67.2 %shard_map.103 = (f32[16,128]{1,0:T(8,128)S(1)}, f32[8,128]{1,0:T(8,128)S(1)}, f32[16,128]{1,0:T(8,128)S(1)}) custom-call(f32[16,128]{1,0:T(8,128)S(1)} %copy-done.1, f32[16,128]{1,0:T(8,128)S(1)} %copy-done.2, f32[16,128]{1,0:T(8,128)S(1)} %copy-done.3, f32[8,128]{1,0:T(8,128)S(1)} %copy-done.4, bf16[32,128,128]{2,1,0:T(8,128)(2,1)S(1)} %copy-done, ...), custom_call_target="tpu_custom_call" | custom-call | tf_op jit(solution)/shard_map/pallas_call | solution.py:313
  71.9 0.6 copy.14
  72.5 0.6 copy.15
  73.1 0.6 copy.16
Async XLA Ops:
  0.6 0.7 copy-start.4
  0.6 0.7 copy-start.5
  0.7 0.7 copy-start.6
  0.7 0.7 copy-start.7
  1.3 1.2 %copy-start = (bf16[32,128,128]{2,1,0:T(8,128)(2,1)S(1)}, bf16[32,128,128]{2,1,0:T(8,128)(2,1)}, u32[]{:S(2)}) copy-start(bf16[32,128,128]{2,1,0:T(8,128)(2,1)} %blocks_hbm.1) | copy-start | bytes 3145732
  2.6 0.7 copy-start.1
  3.3 0.7 copy-start.2
  4.0 0.7 copy-start.3

commit v2 on v1

--- a/solution.py
+++ b/solution.py
@@ -48,14 +48,15 @@
     early_send, early_recv, early_chosen_send, early_chosen_recv,
     norm_a_send, norm_a_recv, norm_b_send, norm_b_recv,
     last_a_send, last_a_recv, last_b_send, last_b_recv,
-    y_send_sem, y_recv_sem, n_send_sem, n_recv_sem, s_send_sem, s_recv_sem,
+    y_send_sem, y_recv_sem, n_send_sem, n_recv_sem, s_send_sem, s_recv_sem, round_sem,
 ):
-    node_count, local_count, row_count = sizes
-    column_count = node_count // row_count
+    node_count, local_count, x_count = sizes
+    z_count = node_count // (2 * x_count)
     node = lax.axis_index("node")
     local = lax.axis_index("local")
-    row = node // column_count
-    column = lax.rem(node, column_count)
+    x = node // (2 * z_count)
+    z = lax.rem(node, 2 * z_count) // 2
+    core = lax.rem(node, 2)
     tiles, block_count = image.shape[0], blocks.shape[0]
     held, owned = ray.shape[1], residual.shape[0]
     rows_sent = node_count * SEND_CAPACITY
@@ -82,38 +83,70 @@
         loads[name] = pltpu.make_async_copy(source, target, load_sem.at[index])
         loads[name].start()
 
-    def of_local(k):
-        other = lax.rem(local + k, local_count)
-        return other, (node, other)
-
-    def of_node(k):
-        other = lax.rem(node + k, node_count)
-        return other, (other, local)
-
-    def of_column(k):
-        other = lax.rem(column + k, column_count)
-        return other, (row * column_count + other, local)
-
-    def of_plane(k):
-        me = row * local_count + local
-        other = lax.rem(me + k, row_count * local_count)
-        return other, (other // local_count * column_count + column, lax.rem(other, local_count))
+    def ring(place, size):
+        def at(i):
+            shift = size // 2 + (i // 2 if i % 2 == 0 else -((i + 1) // 2))
+            return place + shift - jnp.where(place + shift >= size, size, 0)
+
+        return [at(i) for i in range(size)]
+
+    x_ring, core_ring, local_ring = ring(x, x_count), ring(core, 2), ring(local, local_count)
+
+    def z_at(i):
+        shift = z_count // 2 + jnp.where(lax.rem(i, 2) == 0, i // 2, -((i + 1) // 2))
+        return z + shift - jnp.where(z + shift >= z_count, z_count, 0)
+
+    def node_of(x, z, core):
+        return (x * z_count + z) * 2 + core
+
+    def along_z(others, body):
+        def step(i, carry):
+            for other_x, other_core in others:
+                body(other_x, z_at(i), other_core)
+            return carry
+
+        lax.fori_loop(0, z_count - 1, step, 0)
+        for other_x, other_core in others[:-1]:
+            body(other_x, z, other_core)
+
+    def of_local(body):
+        for other in local_ring[:-1]:
+            body(other, (node, other))
+
+    def of_xc(body):
+        for other_x, other_core in [(a, b) for a in x_ring for b in core_ring][:-1]:
+            body(other_x * 2 + other_core, (node_of(other_x, z, other_core), local))
+
+    def of_z(body):
+        along_z([(x, core)], lambda x, z, core: body(z, (node_of(x, z, core), local)))
+
+    def of_node(body):
+        def member(x, z, core):
+            other = node_of(x, z, core)
+            body(other, (other, local))
+
+        along_z([(a, b) for a in x_ring for b in core_ring], member)
+
+    def of_column(body):
+        along_z([(x, b) for b in core_ring], lambda x, z, core: body(z * 2 + core, (node_of(x, z, core), local)))
+
+    def of_plane(body):
+        for other_local, other_x in [(a, b) for a in local_ring for b in x_ring][:-1]:
+            body(other_x * local_count + other_local, (node_of(other_x, z, core), other_local))
 
     local_group = (local_count, local, of_local)
     node_group = (node_count, node, of_node)
-    column_group = (column_count, column, of_column)
-    plane_group = (row_count * local_count, row * local_count + local, of_plane)
-
-    def each(group, body):
-        def step(k, carry):
-            body(*group[2](k))
-            return carry
-
-        lax.fori_loop(1, group[0], step, 0)
+    column_group = (z_count * 2, z * 2 + core, of_column)
+    plane_group = (x_count * local_count, x * local_count + local, of_plane)
 
     barrier = pltpu.get_barrier_semaphore()
-    for group in (local_group, node_group, plane_group):
-        each(group, lambda other, device: pl.semaphore_signal(barrier, inc=1, device_id=device, device_id_type=MESH))
+
+    def greet(semaphore):
+        return lambda other, device: pl.semaphore_signal(semaphore, inc=1, device_id=device, device_id_type=MESH)
+
+    of_local(greet(barrier))
+    of_xc(greet(barrier))
+    of_z(greet(barrier))
 
     def exchange(group, source, target, send_sem, recv_sem):
         def send(other, device):
@@ -122,7 +155,7 @@
                 device_id=device, device_id_type=MESH,
             ).start()
 
-        each(group, send)
+        group[2](send)
         pltpu.make_async_copy(source(group[1]), target, recv_sem).start()
 
     def arrived(buffer, recv_sem):
@@ -160,7 +193,7 @@
             mine = jnp.where(tile_index == pixel[0, b], products[:, i * LANES : (i + 1) * LANES], 0.0)
             contrib_send[pl.ds(b, 1), :] = jnp.sum(mine, axis=0, keepdims=True)
 
-    pl.semaphore_wait(barrier, local_count + node_count + row_count * local_count - 3)
+    pl.semaphore_wait(barrier, local_count + z_count + 2 * x_count - 3)
 
     my_blocks = pl.ds(pl.multiple_of(local * block_count, block_count), block_count)
     my_rows = pl.ds(node * SEND_CAPACITY, SEND_CAPACITY)
@@ -173,6 +206,9 @@
 
     exchange(local_group, lambda other: contrib_send, contrib_recv.at[my_blocks], y_send_sem.at[1], y_recv_sem.at[1])
     exchange(local_group, lambda other: slot_send, slot_recv.at[local], y_send_sem.at[0], y_recv_sem.at[0])
+    of_z(greet(round_sem.at[0]))
+    of_local(greet(round_sem.at[1]))
+    pl.semaphore_wait(round_sem.at[0], z_count - 1)
     exchange(node_group, rows_of(label_send), label_recv.at[my_rows], n_send_sem.at[0], n_recv_sem.at[0])
 
     arrived(slot_recv, y_recv_sem.at[0])
@@ -205,7 +241,7 @@
     exchange(node_group, rows_of(reply_send), reply_recv.at[my_rows], n_send_sem.at[3], n_recv_sem.at[3])
     norm_a_send[0:1, :] = jnp.sum(projected * projected, axis=0, keepdims=True)
     norm_a_send[1:2, :] = old_norm_row
-    exchange(column_group, lambda other: norm_a_send, norm_a_recv.at[column], s_send_sem.at[0], s_recv_sem.at[0])
+    exchange(column_group, lambda other: norm_a_send, norm_a_recv.at[column_group[1]], s_send_sem.at[0], s_recv_sem.at[0])
 
     arrived(early_recv, n_recv_sem.at[2])
     early_chosen_send[...] = one_hot_dot(scatter_rows, early_recv[...])
@@ -216,6 +252,7 @@
     arrived(norm_a_recv, s_recv_sem.at[0])
     norm_b_send[...] = jnp.sum(norm_a_recv[...], axis=0)
     me_in_plane = plane_group[1]
+    pl.semaphore_wait(round_sem.at[1], local_count - 1)
     exchange(plane_group, lambda other: norm_b_send, norm_b_recv.at[me_in_plane], s_send_sem.at[1], s_recv_sem.at[1])
 
     arrived(reply_recv, n_recv_sem.at[3])
@@ -248,7 +285,7 @@
         gradient_new += dot(spread_residual, chunk_blocks)
 
     last_a_send[...] = jnp.sum(gradient_new * gradient_new, axis=0, keepdims=True)
-    exchange(column_group, lambda other: last_a_send, last_a_recv.at[column], s_send_sem.at[2], s_recv_sem.at[2])
+    exchange(column_group, lambda other: last_a_send, last_a_recv.at[column_group[1]], s_send_sem.at[2], s_recv_sem.at[2])
     arrived(last_a_recv, s_recv_sem.at[2])
     last_b_send[...] = jnp.sum(last_a_recv[...], axis=0)
     exchange(plane_group, lambda other: last_b_send, last_b_recv.at[me_in_plane], s_send_sem.at[3], s_recv_sem.at[3])
@@ -274,9 +311,9 @@
 
 def solution(mesh):
     node_count, local_count = mesh.shape["node"], mesh.shape["local"]
-    row_count = 4 if node_count % 4 == 0 and node_count > 4 else 2
-    column_count = node_count // row_count
-    plane_count = row_count * local_count
+    x_count = 4 if node_count % 16 == 0 else 2
+    column_count = node_count // x_count
+    plane_count = x_count * local_count
 
     def on_device(image, direction, gradient, residual, blocks, block_slot, block_pixel, slot_ray):
         rows_sent = node_count * SEND_CAPACITY
@@ -308,16 +345,16 @@
             *pair((2, LANES), (plane_count, 2, LANES)),
             *pair((1, LANES), (column_count, 1, LANES)),
             *pair((1, LANES), (plane_count, 1, LANES)),
-            *[pltpu.SemaphoreType.DMA((4,))] * 6,
+            *[pltpu.SemaphoreType.DMA((4,))] * 6, pltpu.SemaphoreType.REGULAR((2,)),
         ]
         return pl.pallas_call(
-            functools.partial(kernel, (node_count, local_count, row_count)),
+            functools.partial(kernel, (node_count, local_count, x_count)),
             out_shape=tuple(jax.ShapeDtypeStruct(a.shape, jnp.float32) for a in (image, residual, direction)),
-            in_specs=[pl.BlockSpec(memory_space=pl.ANY)] * 8,
+            in_specs=[pl.BlockSpec(memory_space=pltpu.HBM)] * 8,
             out_specs=[pl.BlockSpec(memory_space=pltpu.VMEM)] * 3,
             scratch_shapes=scratch,
             compiler_params=pltpu.CompilerParams(
-                collective_id=0, has_side_effects=True, vmem_limit_bytes=32 * 1024 * 1024
+                collective_id=0, has_side_effects=True, vmem_limit_bytes=60 * 1024 * 1024
             ),
         )(
             image, direction, gradient, residual, blocks,

time: 74 us -> 65 us (0.88)
  Pallas kernels: 67.2 us -> 61.6 us
  local copies, waits for them, and re-layouts: 5.77 us -> 2.6 us
    pallas_call x1, Pallas kernels: 67.2 us -> 61.6 us  [on_device(): pl.pallas_call(functools.partial(kernel, (node_count, local_count, x_coun...]
    unnamed x19 -> x7, local copies, waits for them, and re-layouts: 5.77 us -> 2.6 us
where the time goes in v2:
time: 65 us; the launch traced here: 64.8 us
  Pallas kernels  61.6 us (95%)
  local copies, waits for them, and re-layouts  2.6 us (4%)
  between operations  0.65 us (1%)
    pallas_call x1, Pallas kernels, on_device(): pl.pallas_call(functools.partial(kernel, (node_count, local_count, x_coun...  61.6 us
    unnamed x7, local copies, waits for them, and re-layouts  2.6 us

profile of v2, /device:TPU:1, one launch (start us, length us, event | category | flops | bytes accessed | tf_op | source)
XLA Modules:
  0.0 64.8 jit_solution(5073313451098187208)
XLA Ops:
  0.6 61.6 %shard_map.103 = (f32[16,128]{1,0:T(8,128)}, f32[8,128]{1,0:T(8,128)}, f32[16,128]{1,0:T(8,128)}) custom-call(f32[16,128]{1,0:T(8,128)} %image_hbm.1, f32[16,128]{1,0:T(8,128)} %direction_hbm.1, f32[16,128]{1,0:T(8,128)} %gradient_hbm.1, f32[8,128]{1,0:T(8,128)} %residual_hbm.1, bf16[32,128,128]{2,1,0:T(8,128)(2,1)} %blocks_hbm.1, s32[1,32]{1,0:T(1,128)} %bitcast.3, ...), custom_call_target="tpu_custom_call" | custom-call | tf_op jit(solution)/shard_map/pallas_call | solution.py:350
  62.2 0.0 copy-start.1
  62.2 1.3 %copy.14 = f32[16,128]{1,0:T(8,128)} copy(f32[16,128]{1,0:T(8,128)} %get-tuple-element.6) | data formatting | bytes 16384
  63.5 0.0 copy-done.1
  63.5 0.0 copy-start
  63.5 0.6 copy.15
  64.1 0.1 copy-done
  64.2 0.6 copy.16
Async XLA Ops:
  62.2 1.3 %copy-start.1 = (f32[8,128]{1,0:T(8,128)S(1)}, f32[8,128]{1,0:T(8,128)}, u32[]{:S(2)}) copy-start(f32[8,128]{1,0:T(8,128)} %get-tuple-element.7) | copy-start | bytes 12292
  63.5 0.7 %copy-start = (f32[16,128]{1,0:T(8,128)S(1)}, f32[16,128]{1,0:T(8,128)}, u32[]{:S(2)}) copy-start(f32[16,128]{1,0:T(8,128)} %get-tuple-element.8) | copy-start | bytes 24580

commit v3 on v2

--- a/solution.py
+++ b/solution.py
@@ -62,6 +62,71 @@
     rows_sent = node_count * SEND_CAPACITY
     group_blocks = block_count * local_count
 
+    def ring(place, size):
+        def at(i):
+            shift = size // 2 + (i // 2 if i % 2 == 0 else -((i + 1) // 2))
+            return place + shift - jnp.where(place + shift >= size, size, 0)
+
+        return [at(i) for i in range(size)]
+
+    x_ring, core_ring, local_ring = ring(x, x_count), ring(core, 2), ring(local, local_count)
+
+    def z_at(i):
+        shift = z_count // 2 + jnp.where(lax.rem(i, 2) == 0, i // 2, -((i + 1) // 2))
+        return z + shift - jnp.where(z + shift >= z_count, z_count, 0)
+
+    def node_of(x, z, core):
+        return (x * z_count + z) * 2 + core
+
+    def along_z(others, body):
+        def step(i, carry):
+            for other_x, other_core in others:
+                body(other_x, z_at(i), other_core)
+            return carry
+
+        lax.fori_loop(0, z_count - 1, step, 0)
+        for other_x, other_core in others[:-1]:
+            body(other_x, z, other_core)
+
+    def of_local(body):
+        for other in local_ring[:-1]:
+            body(other, (node, other))
+
+    def of_xc(body):
+        for other_x, other_core in [(a, b) for a in x_ring for b in core_ring][:-1]:
+            body(other_x * 2 + other_core, (node_of(other_x, z, other_core), local))
+
+    def of_z(body):
+        along_z([(x, core)], lambda x, z, core: body(z, (node_of(x, z, core), local)))
+
+    def of_node(body):
+        def member(x, z, core):
+            other = node_of(x, z, core)
+            body(other, (other, local))
+
+        along_z([(a, b) for a in x_ring for b in core_ring], member)
+
+    def of_column(body):
+        along_z([(x, b) for b in core_ring], lambda x, z, core: body(z * 2 + core, (node_of(x, z, core), local)))
+
+    def of_plane(body):
+        for other_local, other_x in [(a, b) for a in local_ring for b in x_ring][:-1]:
+            body(other_x * local_count + other_local, (node_of(other_x, z, core), other_local))
+
+    local_group = (local_count, local, of_local)
+    node_group = (node_count, node, of_node)
+    column_group = (z_count * 2, z * 2 + core, of_column)
+    plane_group = (x_count * local_count, x * local_count + local, of_plane)
+
+    barrier = pltpu.get_barrier_semaphore()
+
+    def greet(semaphore):
+        return lambda other, device: pl.semaphore_signal(semaphore, inc=1, device_id=device, device_id_type=MESH)
+
+    of_z(greet(barrier))
+    of_xc(greet(barrier))
+    of_local(greet(barrier))
+
     chunks = 4
     chunk = block_count // chunks
     loads = {}
@@ -83,71 +148,6 @@
         loads[name] = pltpu.make_async_copy(source, target, load_sem.at[index])
         loads[name].start()
 
-    def ring(place, size):
-        def at(i):
-            shift = size // 2 + (i // 2 if i % 2 == 0 else -((i + 1) // 2))
-            return place + shift - jnp.where(place + shift >= size, size, 0)
-
-        return [at(i) for i in range(size)]
-
-    x_ring, core_ring, local_ring = ring(x, x_count), ring(core, 2), ring(local, local_count)
-
-    def z_at(i):
-        shift = z_count // 2 + jnp.where(lax.rem(i, 2) == 0, i // 2, -((i + 1) // 2))
-        return z + shift - jnp.where(z + shift >= z_count, z_count, 0)
-
-    def node_of(x, z, core):
-        return (x * z_count + z) * 2 + core
-
-    def along_z(others, body):
-        def step(i, carry):
-            for other_x, other_core in others:
-                body(other_x, z_at(i), other_core)
-            return carry
-
-        lax.fori_loop(0, z_count - 1, step, 0)
-        for other_x, other_core in others[:-1]:
-            body(other_x, z, other_core)
-
-    def of_local(body):
-        for other in local_ring[:-1]:
-            body(other, (node, other))
-
-    def of_xc(body):
-        for other_x, other_core in [(a, b) for a in x_ring for b in core_ring][:-1]:
-            body(other_x * 2 + other_core, (node_of(other_x, z, other_core), local))
-
-    def of_z(body):
-        along_z([(x, core)], lambda x, z, core: body(z, (node_of(x, z, core), local)))
-
-    def of_node(body):
-        def member(x, z, core):
-            other = node_of(x, z, core)
-            body(other, (other, local))
-
-        along_z([(a, b) for a in x_ring for b in core_ring], member)
-
-    def of_column(body):
-        along_z([(x, b) for b in core_ring], lambda x, z, core: body(z * 2 + core, (node_of(x, z, core), local)))
-
-    def of_plane(body):
-        for other_local, other_x in [(a, b) for a in local_ring for b in x_ring][:-1]:
-            body(other_x * local_count + other_local, (node_of(other_x, z, core), other_local))
-
-    local_group = (local_count, local, of_local)
-    node_group = (node_count, node, of_node)
-    column_group = (z_count * 2, z * 2 + core, of_column)
-    plane_group = (x_count * local_count, x * local_count + local, of_plane)
-
-    barrier = pltpu.get_barrier_semaphore()
-
-    def greet(semaphore):
-        return lambda other, device: pl.semaphore_signal(semaphore, inc=1, device_id=device, device_id_type=MESH)
-
-    of_local(greet(barrier))
-    of_xc(greet(barrier))
-    of_z(greet(barrier))
-
     def exchange(group, source, target, send_sem, recv_sem):
         def send(other, device):
             pltpu.make_async_remote_copy(
@@ -307,6 +307,12 @@
     sent(plane_group, norm_b_recv, 1, s_send_sem.at[1])
     sent(column_group, last_a_recv, 1, s_send_sem.at[2])
     sent(plane_group, last_b_recv, 1, s_send_sem.at[3])
+
+
+def hand_on(*refs):
+    arrays = len(refs) // 2
+    for i in range(arrays):
+        refs[arrays + i][...] = refs[i][...]
 
 
 def solution(mesh):
@@ -347,7 +353,7 @@
             *pair((1, LANES), (plane_count, 1, LANES)),
             *[pltpu.SemaphoreType.DMA((4,))] * 6, pltpu.SemaphoreType.REGULAR((2,)),
         ]
-        return pl.pallas_call(
+        results = pl.pallas_call(
             functools.partial(kernel, (node_count, local_count, x_count)),
             out_shape=tuple(jax.ShapeDtypeStruct(a.shape, jnp.float32) for a in (image, residual, direction)),
             in_specs=[pl.BlockSpec(memory_space=pltpu.HBM)] * 8,
@@ -361,6 +367,13 @@
             block_slot.reshape(1, block_count), block_pixel.reshape(1, block_count), slot_ray.reshape(1, held),
         )
 
+        return pl.pallas_call(
+            hand_on,
+            out_shape=tuple(jax.ShapeDtypeStruct(a.shape, a.dtype) for a in results),
+            in_specs=[pl.BlockSpec(memory_space=pltpu.VMEM)] * 3,
+            out_specs=[pl.BlockSpec(memory_space=pltpu.VMEM)] * 3,
+        )(*results)
+
     split = P(("node", "local"))
     return jax.shard_map(
         on_device,

time: 65 us -> 63.6 us (0.978)
  local copies, waits for them, and re-layouts: 2.6 us -> 0 us
  Pallas kernels: 61.6 us -> 62.8 us
    unnamed x7 -> x0, local copies, waits for them, and re-layouts: 2.6 us -> none
    pallas_call x0 -> x1, Pallas kernels: none -> 1.33 us  [on_device(): pl.pallas_call(hand_on, out_shape=tuple((jax.ShapeDtypeStruct(a.shape, a....]
where the time goes in v3:
time: 63.6 us; the launch traced here: 63.4 us
  Pallas kernels  62.8 us (99%)
  between operations  0.64 us (1%)
    pallas_call x1, Pallas kernels, on_device(): pl.pallas_call(functools.partial(kernel, (node_count, local_count, x_coun...  61.4 us
    pallas_call x1, Pallas kernels, on_device(): pl.pallas_call(hand_on, out_shape=tuple((jax.ShapeDtypeStruct(a.shape, a....  1.33 us

profile of v3, /device:TPU:1, one launch (start us, length us, event | category | flops | bytes accessed | tf_op | source)
XLA Modules:
  0.0 63.4 jit_solution(12240633526587126268)
XLA Ops:
  0.6 61.4 %shard_map.103 = (f32[16,128]{1,0:T(8,128)}, f32[8,128]{1,0:T(8,128)}, f32[16,128]{1,0:T(8,128)}) custom-call(f32[16,128]{1,0:T(8,128)} %image_hbm.1, f32[16,128]{1,0:T(8,128)} %direction_hbm.1, f32[16,128]{1,0:T(8,128)} %gradient_hbm.1, f32[8,128]{1,0:T(8,128)} %residual_hbm.1, bf16[32,128,128]{2,1,0:T(8,128)(2,1)} %blocks_hbm.1, s32[1,32]{1,0:T(1,128)} %bitcast.3, ...), custom_call_target="tpu_custom_call" | custom-call | tf_op jit(solution)/shard_map/pallas_call | solution.py:356
  62.1 1.3 %shard_map.104 = (f32[16,128]{1,0:T(8,128)}, f32[8,128]{1,0:T(8,128)}, f32[16,128]{1,0:T(8,128)}) custom-call(f32[16,128]{1,0:T(8,128)} %get-tuple-element.6.refs_0_, f32[8,128]{1,0:T(8,128)} %get-tuple-element.7.refs_1_, f32[16,128]{1,0:T(8,128)} %get-tuple-element.8.refs_2_), custom_call_target="tpu_custom_call" | custom-call | tf_op jit(solution)/shard_map/pallas_call | solution.py:370

commit v4 on v3

--- a/solution.py
+++ b/solution.py
@@ -161,6 +161,38 @@
     def arrived(buffer, recv_sem):
         pltpu.make_async_copy(buffer, buffer, recv_sem).wait()
 
+    loads["direction"].wait()
+    loads["pixel"].wait()
+    low_direction = direction[...].astype(jnp.bfloat16)
+    tile_index = iota((tiles, LANES), 0)
+    for c in range(chunks):
+        loads["blocks", c].wait()
+        chunk_blocks = blocks[pl.ds(c * chunk, chunk)].reshape(chunk * LANES, LANES)
+        products = dot(low_direction, chunk_blocks, NT)
+        for i in range(chunk):
+            b = c * chunk + i
+            mine = jnp.where(tile_index == pixel[0, b], products[:, i * LANES : (i + 1) * LANES], 0.0)
+            contrib_send[pl.ds(b, 1), :] = jnp.sum(mine, axis=0, keepdims=True)
+
+    pl.semaphore_wait(barrier, local_count + z_count + 2 * x_count - 3)
+
+    my_blocks = pl.ds(pl.multiple_of(local * block_count, block_count), block_count)
+    my_rows = pl.ds(node * SEND_CAPACITY, SEND_CAPACITY)
+
+    def rows_of(buffer):
+        return lambda other: buffer.at[pl.ds(other * SEND_CAPACITY, SEND_CAPACITY)]
+
+    def blocks_of(buffer):
+        return lambda other: buffer.at[pl.ds(pl.multiple_of(other * block_count, block_count), block_count)]
+
+    exchange(local_group, lambda other: contrib_send, contrib_recv.at[my_blocks], y_send_sem.at[1], y_recv_sem.at[1])
+    loads["slot"].wait()
+    slot_row = jnp.concatenate([slot[...].astype(jnp.float32)] * local_count, axis=1)
+    slot_send[...] = jnp.where(iota(slot_row.shape, 1) // block_count == local, slot_row, 0.0)
+
+    exchange(local_group, lambda other: slot_send, slot_recv.at[local], y_send_sem.at[0], y_recv_sem.at[0])
+    of_z(greet(round_sem.at[0]))
+    of_local(greet(round_sem.at[1]))
     loads["ray"].wait()
     rays = ray[...]
     target_node = lax.div(rays, owned * local_count).astype(jnp.float32)
@@ -176,38 +208,6 @@
     tile_one_hot = (iota((held, LANES), 1).astype(jnp.float32) == to_column(tile)).astype(jnp.bfloat16)
     label_send[...] = dot(spread, tile_one_hot)
 
-    loads["slot"].wait()
-    slot_row = jnp.concatenate([slot[...].astype(jnp.float32)] * local_count, axis=1)
-    slot_send[...] = jnp.where(iota(slot_row.shape, 1) // block_count == local, slot_row, 0.0)
-
-    loads["direction"].wait()
-    loads["pixel"].wait()
-    low_direction = direction[...].astype(jnp.bfloat16)
-    tile_index = iota((tiles, LANES), 0)
-    for c in range(chunks):
-        loads["blocks", c].wait()
-        chunk_blocks = blocks[pl.ds(c * chunk, chunk)].reshape(chunk * LANES, LANES)
-        products = dot(low_direction, chunk_blocks, NT)
-        for i in range(chunk):
-            b = c * chunk + i
-            mine = jnp.where(tile_index == pixel[0, b], products[:, i * LANES : (i + 1) * LANES], 0.0)
-            contrib_send[pl.ds(b, 1), :] = jnp.sum(mine, axis=0, keepdims=True)
-
-    pl.semaphore_wait(barrier, local_count + z_count + 2 * x_count - 3)
-
-    my_blocks = pl.ds(pl.multiple_of(local * block_count, block_count), block_count)
-    my_rows = pl.ds(node * SEND_CAPACITY, SEND_CAPACITY)
-
-    def rows_of(buffer):
-        return lambda other: buffer.at[pl.ds(other * SEND_CAPACITY, SEND_CAPACITY)]
-
-    def blocks_of(buffer):
-        return lambda other: buffer.at[pl.ds(pl.multiple_of(other * block_count, block_count), block_count)]
-
-    exchange(local_group, lambda other: contrib_send, contrib_recv.at[my_blocks], y_send_sem.at[1], y_recv_sem.at[1])
-    exchange(local_group, lambda other: slot_send, slot_recv.at[local], y_send_sem.at[0], y_recv_sem.at[0])
-    of_z(greet(round_sem.at[0]))
-    of_local(greet(round_sem.at[1]))
     pl.semaphore_wait(round_sem.at[0], z_count - 1)
     exchange(node_group, rows_of(label_send), label_recv.at[my_rows], n_send_sem.at[0], n_recv_sem.at[0])
 
@@ -227,6 +227,7 @@
     tile_square = (iota((owned, LANES), 0) == iota((owned, LANES), 1)).astype(jnp.bfloat16)
     collect = dot(tile_square, labels, NT).astype(jnp.bfloat16)
     labels_owned = labels[:, :owned]
+    same_tile = dot(labels_owned, collect).astype(jnp.bfloat16)
     loads["residual"].wait()
     early_send[...] = one_hot_dot(labels_owned, residual[...])
     exchange(node_group, rows_of(early_send), early_recv.at[my_rows], n_send_sem.at[2], n_recv_sem.at[2])
@@ -236,12 +237,12 @@
     old_norm_row = jnp.sum(gradient[...] * gradient[...], axis=0, keepdims=True)
 
     arrived(held_recv, n_recv_sem.at[1])
+    reply_send[...] = one_hot_dot(same_tile, held_recv[...])
     projected = one_hot_dot(collect, held_recv[...])
-    reply_send[...] = one_hot_dot(labels_owned, projected)
-    exchange(node_group, rows_of(reply_send), reply_recv.at[my_rows], n_send_sem.at[3], n_recv_sem.at[3])
     norm_a_send[0:1, :] = jnp.sum(projected * projected, axis=0, keepdims=True)
     norm_a_send[1:2, :] = old_norm_row
     exchange(column_group, lambda other: norm_a_send, norm_a_recv.at[column_group[1]], s_send_sem.at[0], s_recv_sem.at[0])
+    exchange(node_group, rows_of(reply_send), reply_recv.at[my_rows], n_send_sem.at[3], n_recv_sem.at[3])
 
     arrived(early_recv, n_recv_sem.at[2])
     early_chosen_send[...] = one_hot_dot(scatter_rows, early_recv[...])

time: 63.6 us -> 63.6 us (level)
  no operation moved by 1% of the time
where the time goes in v4:
time: 63.6 us; the launch traced here: 63.4 us
  Pallas kernels  62.8 us (99%)
  between operations  0.64 us (1%)
    pallas_call x1, Pallas kernels, on_device(): pl.pallas_call(functools.partial(kernel, (node_count, local_count, x_coun...  61.4 us
    pallas_call x1, Pallas kernels, on_device(): pl.pallas_call(hand_on, out_shape=tuple((jax.ShapeDtypeStruct(a.shape, a....  1.33 us

profile of v4, /device:TPU:1, one launch (start us, length us, event | category | flops | bytes accessed | tf_op | source)
XLA Modules:
  0.0 63.4 jit_solution(3746879830295918569)
XLA Ops:
  0.6 61.4 %shard_map.103 = (f32[16,128]{1,0:T(8,128)}, f32[8,128]{1,0:T(8,128)}, f32[16,128]{1,0:T(8,128)}) custom-call(f32[16,128]{1,0:T(8,128)} %image_hbm.1, f32[16,128]{1,0:T(8,128)} %direction_hbm.1, f32[16,128]{1,0:T(8,128)} %gradient_hbm.1, f32[8,128]{1,0:T(8,128)} %residual_hbm.1, bf16[32,128,128]{2,1,0:T(8,128)(2,1)} %blocks_hbm.1, s32[1,32]{1,0:T(1,128)} %bitcast.3, ...), custom_call_target="tpu_custom_call" | custom-call | tf_op jit(solution)/shard_map/pallas_call | solution.py:357
  62.1 1.3 %shard_map.104 = (f32[16,128]{1,0:T(8,128)}, f32[8,128]{1,0:T(8,128)}, f32[16,128]{1,0:T(8,128)}) custom-call(f32[16,128]{1,0:T(8,128)} %get-tuple-element.6.refs_0_, f32[8,128]{1,0:T(8,128)} %get-tuple-element.7.refs_1_, f32[16,128]{1,0:T(8,128)} %get-tuple-element.8.refs_2_), custom_call_target="tpu_custom_call" | custom-call | tf_op jit(solution)/shard_map/pallas_call | solution.py:371
